TPU v7x, 256 devices: a whole 4x4x8 slice. The times are simulated.
256 devices in a mesh: dp: 4 (over z_lo), space: 8 (over x, z_hi), tensor: 8 (over y, core).
Axes of the slice: x: 4, y: 4, z: 8 (z_hi: 2, z_lo: 4; z = z_hi * 4 + z_lo), core: 2. Of those that a mesh axis runs over, the one named last changes fastest.
Arguments:
- features: bfloat16 [4, 128, 64, 1024], P('dp', ('space', 'tensor')), may hold values from -6 to 6
- kernel: bfloat16 [3, 3, 1024, 1024], P(None, None, 'tensor'), may hold values from -0.0625 to 0.0625
- embedding: float32 [1000, 1024], P(None, 'tensor'), may hold values from -6 to 6
- labels: int32 [4], P('dp'), may hold values from 0 to 999
Outputs:
- weight_grad: float32 [3, 3, 1024, 1024], P(None, None, 'tensor')
- embed_grad: float32 [1000, 1024], P(None, 'tensor')
All inputs are finite; a program needn't handle non-finite values.
Results may differ from a plain program's by a relative error of at most 0.00033.
Values may be sent and summed in bfloat16 or wider, within the bound.
No kernel may reach another device: no remote copies, remote signals or barrier semaphores. Data moves between devices by JAX's collectives and lax.ppermute only.
A program may use at most 64 MiB of HBM per device.

v0:
```python
import math
import jax
import jax.numpy as jnp
from jax import lax
from jax.sharding import PartitionSpec as P

r1_factor = 1000.0


def padded_2(block, sides, width):
    for axis, dim in sides:
        count = lax.axis_size(axis)
        forward = [(i, i + 1) for i in range(count - 1)]
        backward = [(target, source) for source, target in forward]
        low = lax.ppermute(
            lax.slice_in_dim(block, block.shape[dim] - width, None, axis=dim), axis, forward
        )
        high = lax.ppermute(lax.slice_in_dim(block, 0, width, axis=dim), axis, backward)
        block = jnp.concatenate([low, block, high], axis=dim)
    return block


def conv_valid(padded, kern):
    return lax.conv_general_dilated(
        padded,
        kern,
        (1, 1),
        "VALID",
        dimension_numbers=("NHWC", "HWIO", "NHWC"),
        preferred_element_type=jnp.float32,
    )


def pad_cols(field):
    return jnp.pad(field, ((0, 0), (0, 0), (1, 1), (0, 0)))


def taps_of(padded, grad):
    row_count = grad.shape[1]
    col_count = grad.shape[2]
    flat_grad = grad.reshape(-1, grad.shape[3])
    outer = []
    for tap_row in range(3):
        inner = []
        for tap_col in range(3):
            window = padded[
                :, tap_row : tap_row + row_count, tap_col : tap_col + col_count, :
            ].reshape(-1, padded.shape[3])
            inner.append(
                lax.dot_general(
                    window, flat_grad, (((0,), (0,)), ((), ())), preferred_element_type=jnp.float32
                )
            )
        outer.append(jnp.stack(inner))
    return jnp.stack(outer)


def forward_conv(padded, kernel_cols):
    whole = lax.all_gather(padded, "tensor", axis=3, tiled=True)
    return conv_valid(whole, kernel_cols)


def body(features, kernel, embedding, labels):
    tensor_count = lax.axis_size("tensor")
    space_count = lax.axis_size("space")
    image_total = features.shape[0] * lax.axis_size("dp")
    col_count = features.shape[2]
    chan_total = features.shape[3]
    height = features.shape[1] * tensor_count * space_count
    scale = 1.0 / math.sqrt(height * col_count * chan_total)
    gweight = r1_factor / image_total
    local_maps = lax.all_to_all(features, "tensor", split_axis=3, concat_axis=1, tiled=True)
    x_pad = pad_cols(padded_2(local_maps, (("space", 1),), 1))
    kernel_cols = lax.all_to_all(kernel, "tensor", split_axis=3, concat_axis=2, tiled=True)
    hidden = forward_conv(x_pad, kernel_cols)
    class_count = embedding.shape[0]
    onehot = (labels[:, None] == jnp.arange(class_count, dtype=jnp.int32)[None, :]).astype(
        jnp.float32
    )
    embed_rows = jnp.dot(onehot, embedding, precision=lax.Precision.HIGHEST)
    embed_four = embed_rows[:, None, None, :]
    sig = jax.nn.sigmoid(hidden)
    act = hidden * sig
    slope = sig * (1.0 + hidden * (1.0 - sig))
    curve = sig * (1.0 - sig) * (2.0 + hidden * (1.0 - 2.0 * sig))
    score = lax.psum(scale * jnp.sum(act * embed_four, axis=(1, 2, 3)), ("space", "tensor"))
    coeff = -jax.nn.sigmoid(-score) / image_total
    grad_hidden = (embed_four * slope * scale).astype(jnp.bfloat16)
    gh_pad = pad_cols(padded_2(grad_hidden, (("space", 1),), 1))
    flipped = jnp.transpose(kernel[::-1, ::-1], (0, 1, 3, 2))
    gh_whole = lax.all_gather(gh_pad, "tensor", axis=3, tiled=True)
    grad_input = conv_valid(gh_whole, flipped).astype(jnp.bfloat16)
    gx_pad = pad_cols(padded_2(grad_input, (("space", 1),), 1))
    direct = taps_of(gx_pad, gh_whole[:, 1:-1, 1:-1, :])
    second = forward_conv(gx_pad, kernel_cols)
    pre = (
        coeff[:, None, None, None] * embed_four * slope * scale
        + gweight * second * embed_four * curve * scale
    ).astype(jnp.bfloat16)
    adversarial = taps_of(x_pad, lax.all_gather(pre, "tensor", axis=3, tiled=True))
    wgrad = adversarial + gweight * direct
    per_image = coeff[:, None] * scale * jnp.sum(act, axis=(1, 2)) + gweight * scale * jnp.sum(
        second * slope, axis=(1, 2)
    )
    egrad = jnp.dot(onehot.T, per_image, precision=lax.Precision.HIGHEST)
    wtotal, etotal = lax.psum((wgrad, egrad), ("dp", "space"))
    return (wtotal, etotal)


def solution(mesh):
    placed = (
        P("dp", ("space", "tensor"), None, None),
        P(None, None, "tensor", None),
        P(None, "tensor"),
        P("dp"),
    )
    return jax.shard_map(
        body,
        mesh=mesh,
        in_specs=placed,
        out_specs=(P(None, None, "tensor", None), P(None, "tensor")),
        check_vma=False,
    )
```

profile of v0, /device:TPU:1, one launch (start us, length us, event | category | flops | bytes accessed | tf_op | source)
XLA Modules:
  0.0 670.4 jit_solution(11944661111741566787)
XLA Ops:
  7.2 2.1 copy.31
  9.3 1.4 reshape.249
  10.8 12.3 %all_to_all.36 = bf16[8,2,8192]{2,1,0:T(2,128)(2,1)S(1)} all-to-all(bf16[8,2,8192]{2,1,0:T(2,128)(2,1)S(1)} %reshape.249), channel_id=1, replica_groups=mesh['dp'=4,'space'=8,'tensor'=8] {'tensor'}, dimensions={0} | all-to-all | bytes 524288 | tf_op jit(solution)/shard_map/all_to_all | solution.py:72
  26.8 9.4 %collective-permute-start = (bf16[1,1,64,128]{3,2,1,0:T(8,128)(2,1)S(1)}, bf16[1,1,64,128]{3,2,1,0:T(8,128)(2,1)S(1)}, u32[]{:S(2)}, u32[]{:S(2)}) collective-permute-start(bf16[1,1,64,128]{3,2,1,0:T(8,128)(2,1)S(1)} %get-tuple-element.11), channel_id=1, source_target_pairs={{0,8},{8,16},{16,24},{24,32},{32,40},{40,48},{48,56},{1,9},{9,17},... | collective-permute-start | bytes 49160 | tf_op jit(solution)/shard_map/ppermute | solution.py:15
  37.9 3.6 copy.36
  41.5 6.2 all-to-all-start.1
  48.7 47.4 %all-to-all-done.1 = bf16[3,3,128,1024]{2,1,0,3:T(4,128)(2,1)} async-done(((bf16[3,3,128,1024]{2,1,0,3:T(4,128)(2,1)}), bf16[3,3,128,1024]{2,1,0,3:T(4,128)(2,1)}, u32[]{:S(2)}, u32[]{:S(2)}) %all-to-all-start.1) | async-done | bytes 2359328 | tf_op jit(solution)/shard_map/all_to_all | solution.py:74
  96.1 5.6 copy.37
  101.7 3.2 copy.60
  105.5 1.5 copy.35
  107.2 6.5 multiply_convert_fusion
  115.1 9.5 %collective-permute-start.2 = (bf16[1,1,64,128]{3,2,1,0:T(8,128)(2,1)S(1)}, bf16[1,1,64,128]{3,2,1,0:T(8,128)(2,1)S(1)}, u32[]{:S(2)}, u32[]{:S(2)}) collective-permute-start(bf16[1,1,64,128]{3,2,1,0:T(8,128)(2,1)S(1)} %slice.123), channel_id=1, source_target_pairs={{0,8},{8,16},{16,24},{24,32},{32,40},{40,48},{48,56},{1,9},{9,17},... | collective-permute-start | bytes 49160 | tf_op jit(solution)/shard_map/ppermute | solution.py:15
  126.0 39.5 %all-gather.8.cloned.1.call-done = bf16[1,18,66,1024]{3,2,1,0:T(8,128)(2,1)} async-done(((bf16[1,18,66,128]{3,2,1,0:T(8,128)(2,1)}), bf16[1,18,66,1024]{3,2,1,0:T(8,128)(2,1)}) %all-gather.8.cloned.1.call-update) | async-done | bytes 2433040 | tf_op jit(solution)/shard_map/all_gather | solution.py:91
  165.5 3.2 copy.61
  169.2 1.5 copy.44
  170.8 5.7 fusion.81
  178.0 8.0 %collective-permute-start.4 = (bf16[1,1,64,128]{3,2,1,0:T(8,128)(2,1)S(1)}, bf16[1,1,64,128]{3,2,1,0:T(8,128)(2,1)S(1)}, u32[]{:S(2)}, u32[]{:S(2)}) collective-permute-start(bf16[1,1,64,128]{3,2,1,0:T(8,128)(2,1)S(1)} %slice.129), channel_id=1, source_target_pairs={{0,8},{8,16},{16,24},{24,32},{32,40},{40,48},{48,56},{1,9},{9,17},... | collective-permute-start | bytes 49160 | tf_op jit(solution)/shard_map/ppermute | solution.py:15
  188.0 36.1 %all-gather.10.cloned.1.call-done = bf16[1,18,66,1024]{3,2,1,0:T(8,128)(2,1)} async-done(((bf16[1,18,66,128]{3,2,1,0:T(8,128)(2,1)}), bf16[1,18,66,1024]{3,2,1,0:T(8,128)(2,1)}) %all-gather.10.cloned.1.call-update) | async-done | bytes 2433040 | tf_op jit(solution)/shard_map/all_gather | solution.py:59
  224.0 3.2 copy.62
  227.8 1.5 copy.51
  229.6 7.2 %select_reduce_fusion.2 = (f32[128]{0:T(128)S(1)}, f32[128]{0:T(128)S(1)}, f32[]{:T(128)}, f32[16,8,9,128]{3,1,2,0:T(8,128)}) fusion(pred[8,9]{0,1:T(8,128)(4,1)S(1)} %copy-done.17, f32[16,8,9,128]{3,1,2,0:T(8,128)S(1)} %copy-done.15, f32[128]{0:T(128)S(1)} %convolution_bitcast_fusion.9, bf16[3,3,1024,128]{3,2,1,0:T(8,128)(2,1)S(1)} %bitcast.242, ...), kind=kOutput, calls=%fused_computation.90 | convolution fusion | flops 2730147840 | bytes 6710860 | tf_op jit(solution)/shard_map/conv_general_dilated | solution.py:24
  237.5 201.6 %psum.21 = f32[1]{0:T(128)} all-reduce(f32[1]{0:T(128)} %bitcast.13), channel_id=1, replica_groups=mesh['dp'=4,'space'=8,'tensor'=8] {'space','tensor'}, use_global_device_ids=true, to_apply=%region_1.2 | all-reduce | flops 1 | bytes 8 | tf_op jit(solution)/shard_map/psum | solution.py:86
  439.8 1.7 fusion.91
  442.6 1.8 convolution_bitcast_fusion.4
  444.4 1.8 convolution_bitcast_fusion.1
  448.1 1.6 copy-done.7
  453.7 1.9 maximum_bitcast_fusion.3
  456.6 16.8 %all-gather.12.cloned.1.call-done = bf16[16,1,64,1024]{3,2,0,1:T(8,128)(2,1)} async-done(((bf16[16,1,64,128]{3,2,0,1:T(8,128)(2,1)}), bf16[16,1,64,1024]{3,2,0,1:T(8,128)(2,1)}) %all-gather.12.cloned.1.call-update) | async-done | bytes 2097168 | tf_op jit(solution)/shard_map/all_gather | solution.py:100
  473.4 2.2 fusion.69
  481.6 2.7 maximum_add_fusion
  484.3 173.2 %all-reduce.6.cloned.1.call-done = (f32[3,3,128,1024]{3,2,1,0:T(8,128)}, f32[1000,128]{1,0:T(8,128)}) async-done(((f32[3,3,128,1024]{3,2,1,0:T(8,128)}, f32[1000,128]{1,0:T(8,128)}), (f32[3,3,128,1024]{3,2,1,0:T(8,128)}, f32[1000,128]{1,0:T(8,128)})) %all-reduce.6.cloned.1.call-update) | async-done | bytes 5230608 | tf_op jit(solution)/shard_map/psum | solution.py:106
  657.5 5.3 copy.74
  (116 shorter events, 28.6 us)
Async XLA Ops:
  7.2 41.3 %copy-start = (f32[1000,128]{1,0:T(8,128)S(1)}, f32[1000,128]{1,0:T(8,128)}, u32[]{:S(2)}) copy-start(f32[1000,128]{1,0:T(8,128)} %param.6) | copy-start | bytes 1536004
  7.2 30.7 %copy-start.8 = (bf16[3,3,128,1024]{3,2,1,0:T(8,128)(2,1)S(1)}, bf16[3,3,128,1024]{3,2,1,0:T(8,128)(2,1)}, u32[]{:S(2)}) copy-start(bf16[3,3,128,1024]{3,2,1,0:T(8,128)(2,1)} %param.5) | copy-start | bytes 7077892
  7.2 94.5 %all-gather.6.cloned.1.call-start = ((), (), s32[]{:S(2)}) async-start(), calls=%async_computation.2 | async-start | bytes 2985984 | tf_op jit(solution)/shard_map/all_gather | solution.py:59
  25.5 10.8 %collective-permute-start.1 = (bf16[1,1,64,128]{3,2,1,0:T(8,128)(2,1)S(1)}, bf16[1,1,64,128]{3,2,1,0:T(8,128)(2,1)S(1)}, u32[]{:S(2)}, u32[]{:S(2)}) collective-permute-start(bf16[1,1,64,128]{3,2,1,0:T(8,128)(2,1)S(1)} %get-tuple-element.12), channel_id=1, source_target_pairs={{8,0},{16,8},{24,16},{32,24},{40,32},{48,40},{56,48},{9,1},{17,9},... | collective-permute-start | bytes 49160 | tf_op jit(solution)/shard_map/ppermute | solution.py:18
  26.8 10.3 %collective-permute-start = (bf16[1,1,64,128]{3,2,1,0:T(8,128)(2,1)S(1)}, bf16[1,1,64,128]{3,2,1,0:T(8,128)(2,1)S(1)}, u32[]{:S(2)}, u32[]{:S(2)}) collective-permute-start(bf16[1,1,64,128]{3,2,1,0:T(8,128)(2,1)S(1)} %get-tuple-element.11), channel_id=1, source_target_pairs={{0,8},{8,16},{16,24},{24,32},{32,40},{40,48},{48,56},{1,9},{9,17},... | collective-permute-start | bytes 49160 | tf_op jit(solution)/shard_map/ppermute | solution.py:15
  41.5 54.6 %all-to-all-start.1 = ((bf16[3,3,128,1024]{2,1,0,3:T(4,128)(2,1)}), bf16[3,3,128,1024]{2,1,0,3:T(4,128)(2,1)}, u32[]{:S(2)}, u32[]{:S(2)}) async-start(bf16[3,3,128,1024]{2,1,0,3:T(4,128)(2,1)} %copy.36), calls=%async_computation.1 | async-start | bytes 6291456 | tf_op jit(solution)/shard_map/all_to_all | solution.py:74
  47.8 117.7 %all-gather.8.cloned.1.call-start = ((), (), s32[]{:S(2)}) async-start(), calls=%async_computation.3 | async-start | bytes 2985984 | tf_op jit(solution)/shard_map/all_gather | solution.py:91
  105.5 1.7 copy-start.9
  105.5 1.7 copy-start.17
  113.8 11.1 %collective-permute-start.3 = (bf16[1,1,64,128]{3,2,1,0:T(8,128)(2,1)S(1)}, bf16[1,1,64,128]{3,2,1,0:T(8,128)(2,1)S(1)}, u32[]{:S(2)}, u32[]{:S(2)}) collective-permute-start(bf16[1,1,64,128]{3,2,1,0:T(8,128)(2,1)S(1)} %slice.126), channel_id=1, source_target_pairs={{8,0},{16,8},{24,16},{32,24},{40,32},{48,40},{56,48},{9,1},{17,9},... | collective-permute-start | bytes 49160 | tf_op jit(solution)/shard_map/ppermute | solution.py:18
  115.1 9.9 %collective-permute-start.2 = (bf16[1,1,64,128]{3,2,1,0:T(8,128)(2,1)S(1)}, bf16[1,1,64,128]{3,2,1,0:T(8,128)(2,1)S(1)}, u32[]{:S(2)}, u32[]{:S(2)}) collective-permute-start(bf16[1,1,64,128]{3,2,1,0:T(8,128)(2,1)S(1)} %slice.123), channel_id=1, source_target_pairs={{0,8},{8,16},{16,24},{24,32},{32,40},{40,48},{48,56},{1,9},{9,17},... | collective-permute-start | bytes 49160 | tf_op jit(solution)/shard_map/ppermute | solution.py:15
  125.9 98.1 %all-gather.10.cloned.1.call-start = ((), (), s32[]{:S(2)}) async-start(), calls=%async_computation.4 | async-start | bytes 2985984 | tf_op jit(solution)/shard_map/all_gather | solution.py:59
  176.6 10.2 %collective-permute-start.5 = (bf16[1,1,64,128]{3,2,1,0:T(8,128)(2,1)S(1)}, bf16[1,1,64,128]{3,2,1,0:T(8,128)(2,1)S(1)}, u32[]{:S(2)}, u32[]{:S(2)}) collective-permute-start(bf16[1,1,64,128]{3,2,1,0:T(8,128)(2,1)S(1)} %slice.132), channel_id=1, source_target_pairs={{8,0},{16,8},{24,16},{32,24},{40,32},{48,40},{56,48},{9,1},{17,9},... | collective-permute-start | bytes 49160 | tf_op jit(solution)/shard_map/ppermute | solution.py:18
  178.0 8.9 %collective-permute-start.4 = (bf16[1,1,64,128]{3,2,1,0:T(8,128)(2,1)S(1)}, bf16[1,1,64,128]{3,2,1,0:T(8,128)(2,1)S(1)}, u32[]{:S(2)}, u32[]{:S(2)}) collective-permute-start(bf16[1,1,64,128]{3,2,1,0:T(8,128)(2,1)S(1)} %slice.129), channel_id=1, source_target_pairs={{0,8},{8,16},{16,24},{24,32},{32,40},{40,48},{48,56},{1,9},{9,17},... | collective-permute-start | bytes 49160 | tf_op jit(solution)/shard_map/ppermute | solution.py:15
  186.0 0.7 copy-start.14
  186.8 40.4 %copy-start.12 = (bf16[16,1,64,128]{3,2,0,1:T(8,128)(2,1)}, bf16[16,1,64,128]{3,2,0,1:T(8,128)(2,1)S(1)}, u32[]{:S(2)}) copy-start(bf16[16,1,64,128]{3,2,0,1:T(8,128)(2,1)S(1)} %copy.70) | copy-start | bytes 786436
  187.7 285.7 %all-gather.12.cloned.1.call-start = ((), (), s32[]{:S(2)}) async-start(), calls=%async_computation.5 | async-start | bytes 2359296 | tf_op jit(solution)/shard_map/all_gather | solution.py:100
  227.8 1.7 copy-start.10
  227.8 1.8 copy-start.15
  236.8 205.8 %copy-start.6 = (bf16[1,18,66,1024]{3,2,1,0:T(8,128)(2,1)S(1)}, bf16[1,18,66,1024]{3,2,1,0:T(8,128)(2,1)}, u32[]{:S(2)}) copy-start(bf16[1,18,66,1024]{3,2,1,0:T(8,128)(2,1)} %all-gather.8.cloned.1.call-done) | copy-start | bytes 7299076
  442.4 215.2 %all-reduce.6.cloned.1.call-start = ((), (), s32[]{:S(2)}) async-start(), calls=%async_computation.6 | async-start | bytes 10461184 | tf_op jit(solution)/shard_map/psum | solution.py:106
  444.4 1.8 copy-start.11
  447.9 1.8 copy-start.7
  447.9 1.7 copy-start.13
  453.7 19.7 %copy-start.3 = (bf16[1,18,66,128]{3,2,1,0:T(8,128)(2,1)S(1)}, bf16[1,18,66,128]{3,2,1,0:T(8,128)(2,1)}, u32[]{:S(2)}) copy-start(bf16[1,18,66,128]{3,2,1,0:T(8,128)(2,1)} %select_maximum_fusion.4) | copy-start | bytes 912388
  473.4 2.2 copy-start.2
  479.7 1.4 copy-start.4
  479.7 1.9 copy-start.5
  657.5 5.3 copy-start.16
  657.5 6.1 copy-start.1
Sparse Core Ops, SparseCore 0:
  38.0 50.9 all-gather.5
  126.0 39.3 all-gather.7
  187.8 36.1 all-gather.9
  442.5 30.9 all-gather.11
  484.4 173.0 all-reduce.5
where the time goes:
time: 679 us; the launch traced here: 670 us
  waiting for transfers between devices  314 us (46%)
  blocking collectives  214 us (32%)
  local copies, waits for them, and re-layouts  42.6 us (6%)
  starting transfers between devices  37.6 us (6%)
  matrix products  35 us (5%)
  between operations  16.7 us (2%)
  other arithmetic  10.4 us (2%)
    psum x1, blocking collectives, body(): lax.psum(scale * jnp.sum(act * embed_four, axis=(1, 2, 3)), ('space', 'te...  202 us
    psum x1, waiting for transfers between devices, body(): wtotal, etotal = lax.psum((wgrad, egrad), ('dp', 'space'))  173 us
    all_to_all x1, waiting for transfers between devices, body(): lax.all_to_all(kernel, 'tensor', split_axis=3, concat_axis=2, tiled=True)  47.4 us
    all_gather x1, waiting for transfers between devices, body(): gh_whole = lax.all_gather(gh_pad, 'tensor', axis=3, tiled=True)  39.5 us
    all_gather x2, waiting for transfers between devices, forward_conv(): whole = lax.all_gather(padded, 'tensor', axis=3, tiled=True)  36.1 us
    unnamed x48, local copies, waits for them, and re-layouts  28.9 us
    ppermute x3, starting transfers between devices, padded_2(): lax.ppermute(lax.slice_in_dim(block, block.shape[dim] - width, None, axis...  27 us
    conv_general_dilated x3, matrix products, conv_valid(): lax.conv_general_dilated(padded, kern, (1, 1), 'VALID', dimension_numbers...  19.5 us
  transfers between devices with their start and end apart: 12, of which 7 were waited for; matrix products, arithmetic and copies ran while one was open for 3% of the time, Pallas kernels for 0%

commit v1 on v0

--- a/solution.py
+++ b/solution.py
@@ -71,7 +71,26 @@
     gweight = r1_factor / image_total
     local_maps = lax.all_to_all(features, "tensor", split_axis=3, concat_axis=1, tiled=True)
     x_pad = pad_cols(padded_2(local_maps, (("space", 1),), 1))
-    kernel_cols = lax.all_to_all(kernel, "tensor", split_axis=3, concat_axis=2, tiled=True)
+
+    def resolve_series(here_x):
+        carry_out = lax.axis_index("tensor")
+        state_next = lax.axis_size("tensor")
+        current_block, mat_out = (state_next, carry_out)
+        ready = list(here_x.shape)
+        w_next = here_x.shape[3] // current_block
+        ready[3] = w_next
+        f_now = ready[2]
+        ready[2] = f_now * current_block
+        near = jnp.zeros(ready, here_x.dtype)
+        for w in [*range(current_block)]:
+            small = lax.dynamic_slice_in_dim(here_x, (mat_out ^ w) * w_next, w_next, axis=3)
+            if w:
+                current_arr = tuple(((src_i, src_i ^ w) for src_i in range(current_block)))
+                small = lax.ppermute(small, "tensor", current_arr)
+            near = lax.dynamic_update_slice_in_dim(near, small, (mat_out ^ w) * f_now, axis=2)
+        return near
+
+    kernel_cols = resolve_series(kernel)
     hidden = forward_conv(x_pad, kernel_cols)
     class_count = embedding.shape[0]
     onehot = (labels[:, None] == jnp.arange(class_count, dtype=jnp.int32)[None, :]).astype(

time: 679 us -> 661 us (0.973)
  local copies, waits for them, and re-layouts: 42.6 us -> 32.2 us
  waiting for transfers between devices: 314 us -> 305 us
    all_to_all x1 -> x0, waiting for transfers between devices: 47.4 us -> none  [body(): lax.all_to_all(kernel, 'tensor', split_axis=3, concat_axis=2, tiled=True)]
    ppermute x0 -> x7, waiting for transfers between devices: none -> 32.7 us  [resolve_series(): small = lax.ppermute(small, 'tensor', current_arr)]
    ppermute x0 -> x7, starting transfers between devices: none -> 10.5 us  [resolve_series(): small = lax.ppermute(small, 'tensor', current_arr)]
    unnamed x48 -> x43, local copies, waits for them, and re-layouts: 28.9 us -> 22.5 us
  transfers between devices with their start and end apart: 12 -> 18, of which waited for: 7 -> 12; matrix products, arithmetic and copies ran while one was open for 3% -> 2% of each run, Pallas kernels for 0% -> 0%
where the time goes in v1:
time: 661 us; the launch traced here: 655 us
  waiting for transfers between devices  305 us (46%)
  blocking collectives  214 us (32%)
  starting transfers between devices  41.4 us (6%)
  matrix products  35 us (5%)
  local copies, waits for them, and re-layouts  32.2 us (5%)
  between operations  17.1 us (3%)
  other arithmetic  10.4 us (2%)
    psum x1, blocking collectives, body(): lax.psum(scale * jnp.sum(act * embed_four, axis=(1, 2, 3)), ('space', 'te...  202 us
    psum x1, waiting for transfers between devices, body(): wtotal, etotal = lax.psum((wgrad, egrad), ('dp', 'space'))  173 us
    all_gather x2, waiting for transfers between devices, forward_conv(): whole = lax.all_gather(padded, 'tensor', axis=3, tiled=True)  42.4 us
    all_gather x1, waiting for transfers between devices, body(): gh_whole = lax.all_gather(gh_pad, 'tensor', axis=3, tiled=True)  38.6 us
    ppermute x7, waiting for transfers between devices, resolve_series(): small = lax.ppermute(small, 'tensor', current_arr)  32.7 us
    ppermute x3, starting transfers between devices, padded_2(): lax.ppermute(lax.slice_in_dim(block, block.shape[dim] - width, None, axis...  26.1 us
    unnamed x43, local copies, waits for them, and re-layouts  22.5 us
    conv_general_dilated x3, matrix products, conv_valid(): lax.conv_general_dilated(padded, kern, (1, 1), 'VALID', dimension_numbers...  19.5 us
  transfers between devices with their start and end apart: 18, of which 12 were waited for; matrix products, arithmetic and copies ran while one was open for 2% of the time, Pallas kernels for 0%

profile of v1, /device:TPU:1, one launch (start us, length us, event | category | flops | bytes accessed | tf_op | source)
XLA Modules:
  0.0 655.3 jit_solution(9800697105551223320)
XLA Ops:
  8.9 12.3 %all_to_all.18 = bf16[8,2,8192]{2,1,0:T(2,128)(2,1)S(1)} all-to-all(bf16[8,2,8192]{2,1,0:T(2,128)(2,1)S(1)} %reshape.249), channel_id=1, replica_groups=mesh['dp'=4,'space'=8,'tensor'=8] {'tensor'}, dimensions={0} | all-to-all | bytes 524288 | tf_op jit(solution)/shard_map/all_to_all | solution.py:72
  23.2 9.4 %collective-permute-start = (bf16[1,1,64,128]{3,2,1,0:T(8,128)(2,1)S(1)}, bf16[1,1,64,128]{3,2,1,0:T(8,128)(2,1)S(1)}, u32[]{:S(2)}, u32[]{:S(2)}) collective-permute-start(bf16[1,1,64,128]{3,2,1,0:T(8,128)(2,1)S(1)} %get-tuple-element.19), channel_id=1, source_target_pairs={{0,8},{8,16},{16,24},{24,32},{32,40},{40,48},{48,56},{1,9},{9,17},... | collective-permute-start | bytes 49160 | tf_op jit(solution)/shard_map/ppermute | solution.py:15
  34.9 1.8 constant_dynamic-slice_fusion
  36.7 2.0 collective-permute-start.2
  40.9 2.9 collective-permute-start.6
  47.3 2.6 collective-permute-start.8
  49.9 5.4 collective-permute-done.4
  55.3 8.7 %collective-permute-done.5 = bf16[3,3,128,128]{3,2,1,0:T(8,128)(2,1)S(1)} collective-permute-done((bf16[3,3,128,128]{3,2,1,0:T(8,128)(2,1)S(1)}, bf16[3,3,128,128]{3,2,1,0:T(8,128)(2,1)S(1)}, u32[]{:S(2)}, u32[]{:S(2)}) %collective-permute-start.5) | collective-permute-done | bytes 294944 | tf_op jit(solution)/shard_map/ppermute | solution.py:89
  64.1 6.5 collective-permute-done.6
  70.7 10.5 %collective-permute-done.8 = bf16[3,3,128,128]{3,2,1,0:T(8,128)(2,1)S(1)} collective-permute-done((bf16[3,3,128,128]{3,2,1,0:T(8,128)(2,1)S(1)}, bf16[3,3,128,128]{3,2,1,0:T(8,128)(2,1)S(1)}, u32[]{:S(2)}, u32[]{:S(2)}) %collective-permute-start.8) | collective-permute-done | bytes 294944 | tf_op jit(solution)/shard_map/ppermute | solution.py:89
  81.3 6.3 all-gather.6.cloned.1.call-done
  87.6 3.2 copy.56
  93.0 6.5 multiply_convert_fusion
  100.9 8.7 %collective-permute-start.9 = (bf16[1,1,64,128]{3,2,1,0:T(8,128)(2,1)S(1)}, bf16[1,1,64,128]{3,2,1,0:T(8,128)(2,1)S(1)}, u32[]{:S(2)}, u32[]{:S(2)}) collective-permute-start(bf16[1,1,64,128]{3,2,1,0:T(8,128)(2,1)S(1)} %slice.123), channel_id=1, source_target_pairs={{0,8},{8,16},{16,24},{24,32},{32,40},{40,48},{48,56},{1,9},{9,17},... | collective-permute-start | bytes 49160 | tf_op jit(solution)/shard_map/ppermute | solution.py:15
  111.6 38.6 %all-gather.8.cloned.1.call-done = bf16[1,18,66,1024]{3,2,1,0:T(8,128)(2,1)} async-done(((bf16[1,18,66,128]{3,2,1,0:T(8,128)(2,1)}), bf16[1,18,66,1024]{3,2,1,0:T(8,128)(2,1)}) %all-gather.8.cloned.1.call-update) | async-done | bytes 2433040 | tf_op jit(solution)/shard_map/all_gather | solution.py:110
  150.2 3.2 copy.57
  155.6 5.7 fusion.81
  162.7 8.0 %collective-permute-start.11 = (bf16[1,1,64,128]{3,2,1,0:T(8,128)(2,1)S(1)}, bf16[1,1,64,128]{3,2,1,0:T(8,128)(2,1)S(1)}, u32[]{:S(2)}, u32[]{:S(2)}) collective-permute-start(bf16[1,1,64,128]{3,2,1,0:T(8,128)(2,1)S(1)} %slice.129), channel_id=1, source_target_pairs={{0,8},{8,16},{16,24},{24,32},{32,40},{40,48},{48,56},{1,9},{9,17},... | collective-permute-start | bytes 49160 | tf_op jit(solution)/shard_map/ppermute | solution.py:15
  172.7 36.1 %all-gather.10.cloned.1.call-done = bf16[1,18,66,1024]{3,2,1,0:T(8,128)(2,1)} async-done(((bf16[1,18,66,128]{3,2,1,0:T(8,128)(2,1)}), bf16[1,18,66,1024]{3,2,1,0:T(8,128)(2,1)}) %all-gather.10.cloned.1.call-update) | async-done | bytes 2433040 | tf_op jit(solution)/shard_map/all_gather | solution.py:59
  208.8 3.2 copy.58
  214.2 7.3 %select_reduce_fusion.2 = (f32[128]{0:T(128)S(1)}, f32[128]{0:T(128)S(1)}, f32[]{:T(128)}, f32[16,8,9,128]{3,1,2,0:T(8,128)}) fusion(pred[8,9]{0,1:T(8,128)(4,1)S(1)} %copy-done.15, f32[16,8,9,128]{3,1,2,0:T(8,128)S(1)} %copy-done.13, f32[128]{0:T(128)S(1)} %convolution_bitcast_fusion.9, ...), kind=kOutput, calls=%fused_computation.90 | convolution fusion | flops 2730147840 | bytes 6710860 | tf_op jit(solution)/shard_map/conv_general_dilated | solution.py:24
  222.3 201.7 %psum.21 = f32[1]{0:T(128)} all-reduce(f32[1]{0:T(128)} %bitcast.10), channel_id=1, replica_groups=mesh['dp'=4,'space'=8,'tensor'=8] {'space','tensor'}, use_global_device_ids=true, to_apply=%region_1.2 | all-reduce | flops 1 | bytes 8 | tf_op jit(solution)/shard_map/psum | solution.py:105
  424.7 1.7 fusion.91
  427.6 1.8 convolution_bitcast_fusion.4
  429.4 1.8 convolution_bitcast_fusion.1
  433.0 1.6 copy-done.7
  438.7 1.9 maximum_bitcast_fusion.3
  441.6 16.8 %all-gather.12.cloned.1.call-done = bf16[16,1,64,1024]{3,2,0,1:T(8,128)(2,1)} async-done(((bf16[16,1,64,128]{3,2,0,1:T(8,128)(2,1)}), bf16[16,1,64,1024]{3,2,0,1:T(8,128)(2,1)}) %all-gather.12.cloned.1.call-update) | async-done | bytes 2097168 | tf_op jit(solution)/shard_map/all_gather | solution.py:119
  458.4 2.2 fusion.69
  466.5 2.7 maximum_add_fusion
  469.2 173.2 %all-reduce.6.cloned.1.call-done = (f32[3,3,128,1024]{3,2,1,0:T(8,128)}, f32[1000,128]{1,0:T(8,128)}) async-done(((f32[3,3,128,1024]{3,2,1,0:T(8,128)}, f32[1000,128]{1,0:T(8,128)}), (f32[3,3,128,1024]{3,2,1,0:T(8,128)}, f32[1000,128]{1,0:T(8,128)})) %all-reduce.6.cloned.1.call-update) | async-done | bytes 5230608 | tf_op jit(solution)/shard_map/psum | solution.py:125
  642.4 5.3 copy.78
  (131 shorter events, 38.9 us)
Async XLA Ops:
  7.2 37.3 %copy-start = (f32[1000,128]{1,0:T(8,128)S(1)}, f32[1000,128]{1,0:T(8,128)}, u32[]{:S(2)}) copy-start(f32[1000,128]{1,0:T(8,128)} %param.6) | copy-start | bytes 1536004
  7.2 80.4 %all-gather.6.cloned.1.call-start = ((), (), s32[]{:S(2)}) async-start(), calls=%async_computation.1 | async-start | bytes 2985984 | tf_op jit(solution)/shard_map/all_gather | solution.py:59
  21.9 10.8 %collective-permute-start.1 = (bf16[1,1,64,128]{3,2,1,0:T(8,128)(2,1)S(1)}, bf16[1,1,64,128]{3,2,1,0:T(8,128)(2,1)S(1)}, u32[]{:S(2)}, u32[]{:S(2)}) collective-permute-start(bf16[1,1,64,128]{3,2,1,0:T(8,128)(2,1)S(1)} %get-tuple-element.20), channel_id=1, source_target_pairs={{8,0},{16,8},{24,16},{32,24},{40,32},{48,40},{56,48},{9,1},{17,9},... | collective-permute-start | bytes 49160 | tf_op jit(solution)/shard_map/ppermute | solution.py:18
  23.2 10.3 %collective-permute-start = (bf16[1,1,64,128]{3,2,1,0:T(8,128)(2,1)S(1)}, bf16[1,1,64,128]{3,2,1,0:T(8,128)(2,1)S(1)}, u32[]{:S(2)}, u32[]{:S(2)}) collective-permute-start(bf16[1,1,64,128]{3,2,1,0:T(8,128)(2,1)S(1)} %get-tuple-element.19), channel_id=1, source_target_pairs={{0,8},{8,16},{16,24},{24,32},{32,40},{40,48},{48,56},{1,9},{9,17},... | collective-permute-start | bytes 49160 | tf_op jit(solution)/shard_map/ppermute | solution.py:15
  34.4 115.8 %all-gather.8.cloned.1.call-start = ((), (), s32[]{:S(2)}) async-start(), calls=%async_computation.2 | async-start | bytes 2985984 | tf_op jit(solution)/shard_map/all_gather | solution.py:110
  36.7 8.0 %collective-permute-start.2 = (bf16[3,3,128,128]{3,2,1,0:T(8,128)(2,1)S(1)}, bf16[3,3,128,128]{3,2,1,0:T(8,128)(2,1)S(1)}, u32[]{:S(2)}, u32[]{:S(2)}) collective-permute-start(bf16[3,3,128,128]{3,2,1,0:T(8,128)(2,1)S(1)} %get-tuple-element.13), channel_id=1, source_target_pairs={{0,1},{1,0},{2,3},{3,2},{4,5},{5,4},{6,7},{7,6},{8,9},{9,8},{10,11... | collective-permute-start | bytes 884744 | tf_op jit(solution)/shard_map/ppermute | solution.py:89
  38.7 8.6 %collective-permute-start.3 = (bf16[3,3,128,128]{3,2,1,0:T(8,128)(2,1)S(1)}, bf16[3,3,128,128]{3,2,1,0:T(8,128)(2,1)S(1)}, u32[]{:S(2)}, u32[]{:S(2)}) collective-permute-start(bf16[3,3,128,128]{3,2,1,0:T(8,128)(2,1)S(1)} %get-tuple-element.12), channel_id=1, source_target_pairs={{0,2},{1,3},{2,0},{3,1},{4,6},{5,7},{6,4},{7,5},{8,10},{9,11},{10,... | collective-permute-start | bytes 884744 | tf_op jit(solution)/shard_map/ppermute | solution.py:89
  39.0 16.3 %collective-permute-start.4 = (bf16[3,3,128,128]{3,2,1,0:T(8,128)(2,1)S(1)}, bf16[3,3,128,128]{3,2,1,0:T(8,128)(2,1)S(1)}, u32[]{:S(2)}, u32[]{:S(2)}) collective-permute-start(bf16[3,3,128,128]{3,2,1,0:T(8,128)(2,1)S(1)} %get-tuple-element.11), channel_id=1, source_target_pairs={{0,3},{1,2},{2,1},{3,0},{4,7},{5,6},{6,5},{7,4},{8,11},{9,10},{10,... | collective-permute-start | bytes 884744 | tf_op jit(solution)/shard_map/ppermute | solution.py:89
  40.4 23.6 %collective-permute-start.5 = (bf16[3,3,128,128]{3,2,1,0:T(8,128)(2,1)S(1)}, bf16[3,3,128,128]{3,2,1,0:T(8,128)(2,1)S(1)}, u32[]{:S(2)}, u32[]{:S(2)}) collective-permute-start(bf16[3,3,128,128]{3,2,1,0:T(8,128)(2,1)S(1)} %get-tuple-element.10), channel_id=1, source_target_pairs={{0,4},{1,5},{2,6},{3,7},{4,0},{5,1},{6,2},{7,3},{8,12},{9,13},{10,... | collective-permute-start | bytes 884744 | tf_op jit(solution)/shard_map/ppermute | solution.py:89
  40.9 29.8 %collective-permute-start.6 = (bf16[3,3,128,128]{3,2,1,0:T(8,128)(2,1)S(1)}, bf16[3,3,128,128]{3,2,1,0:T(8,128)(2,1)S(1)}, u32[]{:S(2)}, u32[]{:S(2)}) collective-permute-start(bf16[3,3,128,128]{3,2,1,0:T(8,128)(2,1)S(1)} %get-tuple-element.9), channel_id=1, source_target_pairs={{0,5},{1,4},{2,7},{3,6},{4,1},{5,0},{6,3},{7,2},{8,13},{9,12},{10,... | collective-permute-start | bytes 884744 | tf_op jit(solution)/shard_map/ppermute | solution.py:89
  44.7 26.0 %collective-permute-start.7 = (bf16[3,3,128,128]{3,2,1,0:T(8,128)(2,1)S(1)}, bf16[3,3,128,128]{3,2,1,0:T(8,128)(2,1)S(1)}, u32[]{:S(2)}, u32[]{:S(2)}) collective-permute-start(bf16[3,3,128,128]{3,2,1,0:T(8,128)(2,1)S(1)} %get-tuple-element.8), channel_id=1, source_target_pairs={{0,6},{1,7},{2,4},{3,5},{4,2},{5,3},{6,0},{7,1},{8,14},{9,15},{10,... | collective-permute-start | bytes 884744 | tf_op jit(solution)/shard_map/ppermute | solution.py:89
  47.3 34.0 %collective-permute-start.8 = (bf16[3,3,128,128]{3,2,1,0:T(8,128)(2,1)S(1)}, bf16[3,3,128,128]{3,2,1,0:T(8,128)(2,1)S(1)}, u32[]{:S(2)}, u32[]{:S(2)}) collective-permute-start(bf16[3,3,128,128]{3,2,1,0:T(8,128)(2,1)S(1)} %get-tuple-element.7), channel_id=1, source_target_pairs={{0,7},{1,6},{2,5},{3,4},{4,3},{5,2},{6,1},{7,0},{8,15},{9,14},{10,... | collective-permute-start | bytes 884744 | tf_op jit(solution)/shard_map/ppermute | solution.py:89
  91.4 1.6 copy-start.15
  99.6 10.2 %collective-permute-start.10 = (bf16[1,1,64,128]{3,2,1,0:T(8,128)(2,1)S(1)}, bf16[1,1,64,128]{3,2,1,0:T(8,128)(2,1)S(1)}, u32[]{:S(2)}, u32[]{:S(2)}) collective-permute-start(bf16[1,1,64,128]{3,2,1,0:T(8,128)(2,1)S(1)} %slice.126), channel_id=1, source_target_pairs={{8,0},{16,8},{24,16},{32,24},{40,32},{48,40},{56,48},{9,1},{17,9},... | collective-permute-start | bytes 49160 | tf_op jit(solution)/shard_map/ppermute | solution.py:18
  100.9 9.5 %collective-permute-start.9 = (bf16[1,1,64,128]{3,2,1,0:T(8,128)(2,1)S(1)}, bf16[1,1,64,128]{3,2,1,0:T(8,128)(2,1)S(1)}, u32[]{:S(2)}, u32[]{:S(2)}) collective-permute-start(bf16[1,1,64,128]{3,2,1,0:T(8,128)(2,1)S(1)} %slice.123), channel_id=1, source_target_pairs={{0,8},{8,16},{16,24},{24,32},{32,40},{40,48},{48,56},{1,9},{9,17},... | collective-permute-start | bytes 49160 | tf_op jit(solution)/shard_map/ppermute | solution.py:15
  111.3 97.4 %all-gather.10.cloned.1.call-start = ((), (), s32[]{:S(2)}) async-start(), calls=%async_computation.3 | async-start | bytes 2985984 | tf_op jit(solution)/shard_map/all_gather | solution.py:59
  153.9 1.7 copy-start.8
  161.3 10.2 %collective-permute-start.12 = (bf16[1,1,64,128]{3,2,1,0:T(8,128)(2,1)S(1)}, bf16[1,1,64,128]{3,2,1,0:T(8,128)(2,1)S(1)}, u32[]{:S(2)}, u32[]{:S(2)}) collective-permute-start(bf16[1,1,64,128]{3,2,1,0:T(8,128)(2,1)S(1)} %slice.132), channel_id=1, source_target_pairs={{8,0},{16,8},{24,16},{32,24},{40,32},{48,40},{56,48},{9,1},{17,9},... | collective-permute-start | bytes 49160 | tf_op jit(solution)/shard_map/ppermute | solution.py:18
  162.7 8.9 %collective-permute-start.11 = (bf16[1,1,64,128]{3,2,1,0:T(8,128)(2,1)S(1)}, bf16[1,1,64,128]{3,2,1,0:T(8,128)(2,1)S(1)}, u32[]{:S(2)}, u32[]{:S(2)}) collective-permute-start(bf16[1,1,64,128]{3,2,1,0:T(8,128)(2,1)S(1)} %slice.129), channel_id=1, source_target_pairs={{0,8},{8,16},{16,24},{24,32},{32,40},{40,48},{48,56},{1,9},{9,17},... | collective-permute-start | bytes 49160 | tf_op jit(solution)/shard_map/ppermute | solution.py:15
  171.5 40.4 %copy-start.10 = (bf16[16,1,64,128]{3,2,0,1:T(8,128)(2,1)}, bf16[16,1,64,128]{3,2,0,1:T(8,128)(2,1)S(1)}, u32[]{:S(2)}) copy-start(bf16[16,1,64,128]{3,2,0,1:T(8,128)(2,1)S(1)} %copy.66) | copy-start | bytes 786436
  172.4 285.9 %all-gather.12.cloned.1.call-start = ((), (), s32[]{:S(2)}) async-start(), calls=%async_computation.4 | async-start | bytes 2359296 | tf_op jit(solution)/shard_map/all_gather | solution.py:119
  212.5 1.6 copy-start.13
  221.4 206.1 %copy-start.6 = (bf16[1,18,66,1024]{3,2,1,0:T(8,128)(2,1)S(1)}, bf16[1,18,66,1024]{3,2,1,0:T(8,128)(2,1)}, u32[]{:S(2)}) copy-start(bf16[1,18,66,1024]{3,2,1,0:T(8,128)(2,1)} %all-gather.8.cloned.1.call-done) | copy-start | bytes 7299076
  427.3 215.1 %all-reduce.6.cloned.1.call-start = ((), (), s32[]{:S(2)}) async-start(), calls=%async_computation.5 | async-start | bytes 10461184 | tf_op jit(solution)/shard_map/psum | solution.py:125
  429.4 1.8 copy-start.9
  432.8 1.8 copy-start.7
  432.8 1.7 copy-start.11
  438.6 19.7 %copy-start.3 = (bf16[1,18,66,128]{3,2,1,0:T(8,128)(2,1)S(1)}, bf16[1,18,66,128]{3,2,1,0:T(8,128)(2,1)}, u32[]{:S(2)}) copy-start(bf16[1,18,66,128]{3,2,1,0:T(8,128)(2,1)} %select_maximum_fusion.4) | copy-start | bytes 912388
  458.3 2.2 copy-start.2
  464.6 1.9 copy-start.5
  642.4 5.3 copy-start.14
  642.4 6.1 copy-start.1
  (2 other events, 2.1 us)
Sparse Core Ops, SparseCore 0:
  34.5 53.0 all-gather.5
  111.5 38.6 all-gather.7
  172.6 36.1 all-gather.9
  427.4 30.9 all-gather.11
  469.3 173.0 all-reduce.5
